TPU v7x, 256 devices: a whole 4x4x8 slice. The times are simulated.
256 devices in a mesh: row: 8 (over x, core), col: 32 (over y, z).
Axes of the slice: x: 4, y: 4, z: 8, core: 2. Of those that a mesh axis runs over, the one named last changes fastest.
Arguments:
- features: bfloat16 [65536, 256], P(('row', 'col')), may hold values from -6 to 6
- neighbours: int32 [10, 65536], P(None, ('row', 'col')), may hold values from 0 to 511, as said below
- halo_ids: int32 [256, 1, 256], P(('row', 'col')), may hold values from 0 to 255
- w_self: bfloat16 [256, 256], replicated, may hold values from -0.375 to 0.375
- w_neigh: bfloat16 [256, 256], replicated, may hold values from -0.75 to 0.75
- b_sage: float32 [256], replicated, may hold values from -3 to 3
- w_first: bfloat16 [512, 256], replicated, may hold values from -0.25 to 0.25
- b_first: float32 [256], replicated, may hold values from -3 to 3
- w_second: bfloat16 [256], replicated, may hold values from -1.5 to 1.5
- b_second: float32 [1], replicated, may hold values from -3 to 3
- src_owner: int32 [8, 32, 8192, 1], P('row', 'col'), may hold values from 0 to 31; in each aligned block of 8192 rows (0 to 8191, 8192 to 16383, ..., all dimensions but the last counted through in order) at most 320 rows name the same one
- src_local: int32 [8, 32, 8192], P('row', 'col'), may hold values from 0 to 255
- dst_index: int32 [8, 32, 8192], P('row', 'col'), may hold values from 0 to 2047
- labels: int32 [8, 32, 8192], P('row', 'col'), may hold values 0 or 1
Outputs:
- embeds: bfloat16 [65536, 256], P(('row', 'col'))
- logits: float32 [8, 32, 8192], P('row', 'col')
- node_grad: float32 [65536, 256], P(('row', 'col'))
- grad_self: float32 [256, 256], replicated
- grad_neigh: float32 [256, 256], replicated
- grad_bsage: float32 [256], replicated
- grad_first: float32 [32, 512, 256], P('col')
- grad_bfirst: float32 [32, 256], P('col')
- grad_second: float32 [32, 256], P('col')
Inputs may be any that keep to these rules, and one draw needn't show every extreme that they name: `neighbours`: in each partition every one of the 256 received rows (values 256 and up) is named by exactly one entry; the other entries name the partition's own rows. `src_owner`: among the 8192 edges of one tile at most 320 name the same source partition, and that many are reached.
All inputs are finite; a program needn't handle non-finite values. No bound on the sum of `labels` on one device may be relied on, other than what follows from the above.
Results may differ from a plain program's by a relative error of at most 0.0052.
Values may be sent and summed in bfloat16 or wider, within the bound.
No kernel may reach another device: no remote copies, remote signals or barrier semaphores. Data moves between devices by JAX's collectives and lax.ppermute only.
A program may use at most 128 MiB of HBM per device.

v0:
```python
import jax
import jax.numpy as jnp
from jax import lax
from jax.sharding import PartitionSpec as P


def per_device(
    features,
    neighbours,
    halo_ids,
    w_self,
    w_neigh,
    b_sage,
    w_first,
    b_first,
    w_second,
    b_second,
    src_owner,
    src_local,
    dst_index,
    labels,
):
    node_dev, feat_width = features.shape
    fanout = neighbours.shape[0]
    row_count = lax.axis_size("row")
    col_count = lax.axis_size("col")
    outgoing = features[halo_ids[0]]
    halo_count = outgoing.shape[0]
    outgoing = outgoing.reshape(halo_count, row_count, col_count, feat_width)
    received = lax.all_to_all(
        lax.all_to_all(outgoing, "row", split_axis=1, concat_axis=1, tiled=True),
        "col",
        split_axis=2,
        concat_axis=2,
        tiled=True,
    )
    extended = jnp.concatenate([features, received.reshape(-1, feat_width)], axis=0)
    gathered = extended[neighbours].astype(jnp.float32)
    aggregate = (jnp.sum(gathered, axis=0) / fanout).astype(jnp.bfloat16)
    embed_f = jnp.dot(features, w_self, preferred_element_type=jnp.float32)
    embed_f = embed_f + jnp.dot(aggregate, w_neigh, preferred_element_type=jnp.float32) + b_sage
    embeds = embed_f.astype(jnp.bfloat16)
    owners = src_owner[0, 0, :, 0]
    local_rows = src_local[0, 0]
    dest_rows = dst_index[0, 0]
    targets = labels[0, 0].astype(jnp.float32)
    edge_count = owners.shape[0]
    src_block = lax.all_gather(embeds, "col", axis=0, tiled=True)
    block_rows = owners * node_dev + local_rows
    src_embed = src_block[block_rows]
    dst_block = lax.all_gather(embeds, "row", axis=0, tiled=True)
    dst_embed = dst_block[dest_rows]
    w_src = w_first[:feat_width]
    w_dst = w_first[feat_width:]
    preact = jnp.dot(src_embed, w_src, preferred_element_type=jnp.float32)
    preact = preact + jnp.dot(dst_embed, w_dst, preferred_element_type=jnp.float32) + b_first
    gate_sig = jax.nn.sigmoid(preact)
    hidden = preact * gate_sig
    hidden_b = hidden.astype(jnp.bfloat16)
    logits = jnp.dot(hidden_b, w_second, preferred_element_type=jnp.float32) + b_second[0]
    dlogit = jax.nn.sigmoid(logits) - targets
    second_f = w_second.astype(jnp.float32)
    dpreact = dlogit[:, None] * second_f[None, :] * gate_sig * (1.0 + preact * (1.0 - gate_sig))
    dpreact_b = dpreact.astype(jnp.bfloat16)
    part_second = jnp.sum(hidden * dlogit[:, None], axis=0)
    part_bfirst = jnp.sum(dpreact, axis=0)
    grad_src = jnp.dot(src_embed.T, dpreact_b, preferred_element_type=jnp.float32)
    grad_dst = jnp.dot(dst_embed.T, dpreact_b, preferred_element_type=jnp.float32)
    part_first = jnp.concatenate([grad_src, grad_dst], axis=0)
    decoder_sums = lax.psum((part_first, part_bfirst, part_second), "row")
    src_rows_g = jnp.dot(dpreact_b, w_src.T, preferred_element_type=jnp.float32).astype(
        jnp.bfloat16
    )
    dst_rows_g = jnp.dot(dpreact_b, w_dst.T, preferred_element_type=jnp.float32).astype(
        jnp.bfloat16
    )
    src_acc = (
        jnp.zeros((src_block.shape[0], feat_width), jnp.float32)
        .at[block_rows]
        .add(src_rows_g.astype(jnp.float32))
    )
    src_grad = lax.psum_scatter(src_acc, "col", scatter_dimension=0, tiled=True)
    dest_acc = (
        jnp.zeros((dst_block.shape[0], feat_width), jnp.float32)
        .at[dest_rows]
        .add(dst_rows_g.astype(jnp.float32))
    )
    dest_grad = lax.psum_scatter(dest_acc, "row", scatter_dimension=0, tiled=True)
    node_grad = src_grad + dest_grad
    node_grad_b = node_grad.astype(jnp.bfloat16)
    part_self = jnp.dot(features.T, node_grad_b, preferred_element_type=jnp.float32)
    part_neigh = jnp.dot(aggregate.T, node_grad_b, preferred_element_type=jnp.float32)
    part_bsage = jnp.sum(node_grad, axis=0)
    encoder_sums = lax.psum((part_self, part_neigh, part_bsage), ("row", "col"))
    return (
        embeds,
        logits.reshape(1, 1, edge_count),
        node_grad,
        encoder_sums[0],
        encoder_sums[1],
        encoder_sums[2],
        decoder_sums[0][None],
        decoder_sums[1][None],
        decoder_sums[2][None],
    )


def solution(mesh):
    placed = (
        P(("row", "col"), None),
        P(None, ("row", "col")),
        P(("row", "col"), None, None),
        P(),
        P(),
        P(),
        P(),
        P(),
        P(),
        P(),
        P("row", "col", None, None),
        P("row", "col", None),
        P("row", "col", None),
        P("row", "col", None),
    )
    return jax.shard_map(
        per_device,
        mesh=mesh,
        in_specs=placed,
        out_specs=(
            P(("row", "col"), None),
            P("row", "col", None),
            P(("row", "col"), None),
            P(),
            P(),
            P(),
            P("col", None, None),
            P("col", None),
            P("col", None),
        ),
        check_vma=False,
    )
```

profile of v0, /device:TPU:8, one launch (start us, length us, event | category | flops | bytes accessed | tf_op | source)
XLA Modules:
  0.0 875.0 jit_solution(14454785513505962907)
XLA Ops:
  8.0 2.5 gather_fusion
  10.5 4.4 all-to-all-start
  15.7 5.4 all-to-all-done
  21.8 11.7 %all-to-all-start.1 = ((bf16[1,8,32,256]{3,1,0,2:T(8,128)(2,1)}), bf16[1,8,32,256]{3,1,0,2:T(8,128)(2,1)S(1)}, u32[]{:S(2)}, u32[]{:S(2)}) async-start(bf16[1,8,32,256]{3,1,0,2:T(8,128)(2,1)} %copy.26), calls=%async_computation.1 | async-start | bytes 262144 | tf_op jit(solution)/shard_map/all_to_all | solution.py:30
  33.6 1.1 fusion.26
  34.7 7.9 all-to-all-done.1
  43.6 7.6 gather_fusion.1
  54.1 18.4 %all-gather.5.cloned.1.call-done = bf16[2048,256]{1,0:T(8,128)(2,1)} async-done(((bf16[256,256]{1,0:T(8,128)(2,1)}), bf16[2048,256]{1,0:T(8,128)(2,1)}) %all-gather.5.cloned.1.call-update) | async-done | bytes 1048592 | tf_op jit(solution)/shard_map/all_gather | solution.py:51
  72.6 32.2 %gather_fusion.3 = bf16[8192,256]{1,0:T(8,128)(2,1)} fusion(bf16[2048,256]{1,0:T(8,128)(2,1)} %all-gather.5.cloned.1.call-done, s32[8192]{0:T(1024)S(1)} %broadcast_clamp_fusion), kind=kCustom, calls=%fused_computation.3 | custom fusion | bytes 8421376 | tf_op jit(solution)/shard_map/gather | solution.py:52
  104.8 51.4 %all-gather.3.cloned.1.call-done = bf16[8192,256]{1,0:T(8,128)(2,1)} async-done(((bf16[256,256]{1,0:T(8,128)(2,1)}), bf16[8192,256]{1,0:T(8,128)(2,1)}) %all-gather.3.cloned.1.call-update) | async-done | bytes 4194320 | tf_op jit(solution)/shard_map/all_gather | solution.py:48
  156.2 33.6 %gather_fusion.2 = bf16[8192,256]{1,0:T(8,128)(2,1)} fusion(bf16[8192,256]{1,0:T(8,128)(2,1)} %all-gather.3.cloned.1.call-done, s32[8192]{0:T(1024)S(1)} %broadcast_clamp_fusion.1), kind=kCustom, calls=%fused_computation.2 | custom fusion | bytes 8421376 | tf_op jit(solution)/shard_map/gather | solution.py:50
  189.8 3.6 fusion.16
  193.4 1.3 fusion
  194.7 2.4 fusion.6
  197.8 5.9 fusion.24
  203.6 2.0 copy-done.2
  205.6 4.5 fusion.1
  210.1 46.0 %scatter_custom_fusion.1 = f32[2048,256]{1,0:T(8,128)} fusion(s32[8192]{0:T(1024)S(1)} %bitcast.48, f32[8192,256]{1,0:T(8,128)} %fusion.1, f32[]{:T(128)} %constant.11.clone.1), kind=kCustom, calls=%fused_computation.25 | custom fusion | flops 2097152 | bytes 2097664 | tf_op jit(solution)/shard_map/scatter-add | solution.py:86
  256.4 6.7 fusion.2
  263.1 48.3 %scatter_custom_fusion = f32[8192,256]{1,0:T(8,128)} fusion(s32[8192]{0:T(1024)S(1)} %bitcast.46, f32[8192,256]{1,0:T(8,128)} %fusion.2, f32[]{:T(128)} %constant.11.clone.1), kind=kCustom, calls=%fused_computation.16 | custom fusion | flops 2097152 | bytes 8389120 | tf_op jit(solution)/shard_map/scatter-add | solution.py:80
  311.5 4.8 fusion.27
  316.3 221.9 %reduce-scatter.3.cloned.1.call-done = f32[256,256]{1,0:T(8,128)} async-done(((f32[8192,256]{1,0:T(8,128)}), f32[256,256]{1,0:T(8,128)}) %reduce-scatter.3.cloned.1.call-update) | async-done | bytes 262160 | tf_op jit(solution)/shard_map/reduce_scatter | solution.py:82
  538.3 1.1 fusion.25
  539.4 0.9 fusion.18
  541.3 4.8 fusion.28
  547.0 13.0 %all-reduce.1 = (f32[1,256]{1,0:T(1,128)}, f32[1,256]{1,0:T(1,128)}) all-reduce(f32[1,256]{1,0:T(1,128)S(1)} %bitcast.52, f32[1,256]{1,0:T(1,128)S(1)} %bitcast.53), channel_id=1, replica_groups=mesh['row'=8,'col'=32] {'row'}, use_global_device_ids=true, to_apply=%region_11.0 | all-reduce | flops 512 | bytes 4096 | tf_op jit(solution)/shard_map/psum | solution.py:70
  560.0 74.7 %psum.44 = f32[256]{0:T(256)} all-reduce(f32[256]{0:T(256)S(1)} %get-tuple-element.42), channel_id=1, replica_groups=mesh['row'=8,'col'=32] {'row','col'}, use_global_device_ids=true, to_apply=%region_8.0 | all-reduce | flops 256 | bytes 2048 | tf_op jit(solution)/shard_map/psum | solution.py:94
  634.6 162.6 %all-reduce.7.cloned.1.call-done = (f32[256,256]{0,1:T(8,128)}, f32[256,256]{1,0:T(8,128)}) async-done(((f32[256,256]{0,1:T(8,128)}, f32[256,256]{1,0:T(8,128)}), (f32[256,256]{0,1:T(8,128)}, f32[256,256]{1,0:T(8,128)})) %all-reduce.7.cloned.1.call-update) | async-done | bytes 524304 | tf_op jit(solution)/shard_map/psum | solution.py:94
  797.2 1.8 copy.28
  799.0 65.6 %all-reduce.5.cloned.1.call-done = f32[1,512,256]{2,1,0:T(8,128)} async-done(((f32[1,512,256]{2,1,0:T(8,128)}), f32[1,512,256]{2,1,0:T(8,128)}) %all-reduce.5.cloned.1.call-update) | async-done | bytes 524304 | tf_op jit(solution)/shard_map/psum | solution.py:70
  864.6 1.7 copy.33
  866.2 1.9 copy.34
  (62 shorter events, 8.2 us)
Async XLA Ops:
  7.2 26.4 %copy-start = (bf16[256,256]{1,0:T(8,128)(2,1)S(1)}, bf16[256,256]{1,0:T(8,128)(2,1)}, u32[]{:S(2)}) copy-start(bf16[256,256]{1,0:T(8,128)(2,1)} %param.17) | copy-start | bytes 393220
  7.2 44.2 %copy-start.13 = (f32[256]{0:T(256)S(1)}, f32[256]{0:T(256)}, u32[]{:S(2)}) copy-start(f32[256]{0:T(256)} %param.19) | copy-start | bytes 3076
  7.2 44.2 %copy-start.7 = (bf16[256,256]{1,0:T(8,128)(2,1)S(1)}, bf16[256,256]{1,0:T(8,128)(2,1)}, u32[]{:S(2)}) copy-start(bf16[256,256]{1,0:T(8,128)(2,1)} %param.18) | copy-start | bytes 393220
  10.5 42.7 %copy-start.14 = (bf16[256]{0:T(256)(128)(2,1)S(1)}, bf16[256]{0:T(256)(128)(2,1)}, u32[]{:S(2)}) copy-start(bf16[256]{0:T(256)(128)(2,1)} %param.22) | copy-start | bytes 1540
  10.5 43.4 %copy-start.10 = (s32[1,1,8192]{2,1,0:T(1,128)S(1)}, s32[1,1,8192]{2,1,0:T(1,128)}, u32[]{:S(2)}) copy-start(s32[1,1,8192]{2,1,0:T(1,128)} %param.27) | copy-start | bytes 98308
  10.5 43.4 %copy-start.8 = (s32[1,1,8192]{2,1,0:T(1,128)S(1)}, s32[1,1,8192]{2,1,0:T(1,128)}, u32[]{:S(2)}) copy-start(s32[1,1,8192]{2,1,0:T(1,128)} %param.25) | copy-start | bytes 98308
  10.5 43.5 %copy-start.9 = (s32[1,1,8192,1]{2,3,1,0:T(1,128)S(1)}, s32[1,1,8192,1]{2,3,1,0:T(1,128)}, u32[]{:S(2)}) copy-start(s32[1,1,8192,1]{2,3,1,0:T(1,128)} %param.24) | copy-start | bytes 98308
  10.5 43.5 %copy-start.11 = (s32[1,1,8192]{2,1,0:T(1,128)S(1)}, s32[1,1,8192]{2,1,0:T(1,128)}, u32[]{:S(2)}) copy-start(s32[1,1,8192]{2,1,0:T(1,128)} %param.26) | copy-start | bytes 98308
  10.5 10.6 %all-to-all-start = ((bf16[1,8,32,256]{3,2,0,1:T(8,128)(2,1)}), bf16[1,8,32,256]{3,2,0,1:T(8,128)(2,1)S(1)}, u32[]{:S(2)}, u32[]{:S(2)}) async-start(bf16[1,8,32,256]{3,2,0,1:T(8,128)(2,1)} %bitcast.3), calls=%async_computation | async-start | bytes 262144 | tf_op jit(solution)/shard_map/all_to_all | solution.py:31
  21.8 20.8 %all-to-all-start.1 = ((bf16[1,8,32,256]{3,1,0,2:T(8,128)(2,1)}), bf16[1,8,32,256]{3,1,0,2:T(8,128)(2,1)S(1)}, u32[]{:S(2)}, u32[]{:S(2)}) async-start(bf16[1,8,32,256]{3,1,0,2:T(8,128)(2,1)} %copy.26), calls=%async_computation.1 | async-start | bytes 262144 | tf_op jit(solution)/shard_map/all_to_all | solution.py:30
  33.6 39.0 %all-gather.5.cloned.1.call-start = ((), (), s32[]{:S(2)}) async-start(), calls=%async_computation.5 | async-start | bytes 1179648 | tf_op jit(solution)/shard_map/all_gather | solution.py:51
  52.3 103.9 %all-gather.3.cloned.1.call-start = ((), (), s32[]{:S(2)}) async-start(), calls=%async_computation.4 | async-start | bytes 4325376 | tf_op jit(solution)/shard_map/all_gather | solution.py:48
  53.0 263.3 %reduce-scatter.5.cloned.1.call-start = ((), (), s32[]{:S(2)}) async-start(), calls=%async_computation.7 | async-start | bytes 2359296 | tf_op jit(solution)/shard_map/reduce_scatter | solution.py:88
  104.8 85.0 %copy-start.6 = (bf16[512,256]{1,0:T(8,128)(2,1)S(1)}, bf16[512,256]{1,0:T(8,128)(2,1)}, u32[]{:S(2)}) copy-start(bf16[512,256]{1,0:T(8,128)(2,1)} %param.20) | copy-start | bytes 786436
  189.8 3.6 copy-start.3
  189.8 3.6 copy-start.12
  203.6 2.0 copy-start.2
  256.2 282.1 %reduce-scatter.3.cloned.1.call-start = ((), (), s32[]{:S(2)}) async-start(), calls=%async_computation.6 | async-start | bytes 8650752 | tf_op jit(solution)/shard_map/reduce_scatter | solution.py:82
  311.5 228.8 %copy-start.4 = (bf16[256,256]{1,0:T(8,128)(2,1)S(1)}, bf16[256,256]{1,0:T(8,128)(2,1)}, u32[]{:S(2)}) copy-start(bf16[256,256]{1,0:T(8,128)(2,1)} %param.14) | copy-start | bytes 393220
  311.5 485.7 %all-reduce.7.cloned.1.call-start = ((), (), s32[]{:S(2)}) async-start(), calls=%async_computation.9 | async-start | bytes 1048576 | tf_op jit(solution)/shard_map/psum | solution.py:94
  539.4 6.7 copy-start.5
  541.3 326.8 %copy-start.1 = (bf16[256,256]{1,0:T(8,128)(2,1)S(1)}, bf16[256,256]{1,0:T(8,128)(2,1)}, u32[]{:S(2)}) copy-start(bf16[256,256]{1,0:T(8,128)(2,1)} %param.17) | copy-start | bytes 393220
  541.3 323.3 %all-reduce.5.cloned.1.call-start = ((), (), s32[]{:S(2)}) async-start(), calls=%async_computation.8 | async-start | bytes 1048576 | tf_op jit(solution)/shard_map/psum | solution.py:70
Sparse Core Ops, SparseCore 0:
  52.4 20.1 all-gather.4
  75.7 80.4 all-gather.2
  256.3 34.6 reduce-scatter.4
  311.6 226.6 reduce-scatter.2
  545.3 251.9 all-reduce.6
  800.1 64.4 all-reduce.4
where the time goes:
time: 876 us; the launch traced here: 875 us
  waiting for transfers between devices  534 us (61%)
  other arithmetic  105 us (12%)
  blocking collectives  87.7 us (10%)
  local copies, waits for them, and re-layouts  84.1 us (10%)
  matrix products  31.8 us (4%)
  starting transfers between devices  16.8 us (2%)
  between operations  15.1 us (2%)
    reduce_scatter x1, waiting for transfers between devices, per_device(): src_grad = lax.psum_scatter(src_acc, 'col', scatter_dimension=0, tiled=True)  222 us
    psum x1, waiting for transfers between devices, per_device(): encoder_sums = lax.psum((part_self, part_neigh, part_bsage), ('row', 'col'))  163 us
    psum x1, blocking collectives, per_device(): encoder_sums = lax.psum((part_self, part_neigh, part_bsage), ('row', 'col'))  74.7 us
    psum x1, waiting for transfers between devices, per_device(): decoder_sums = lax.psum((part_first, part_bfirst, part_second), 'row')  65.6 us
    all_gather x1, waiting for transfers between devices, per_device(): src_block = lax.all_gather(embeds, 'col', axis=0, tiled=True)  51.4 us
    scatter-add x1, other arithmetic, per_device(): src_acc = jnp.zeros((src_block.shape[0], feat_width), jnp.float32).at[blo...  48.3 us
    scatter-add x1, other arithmetic, per_device(): dest_acc = jnp.zeros((dst_block.shape[0], feat_width), jnp.float32).at[de...  46 us
    gather x1, local copies, waits for them, and re-layouts, per_device(): src_embed = src_block[block_rows]  33.6 us
  transfers between devices with their start and end apart: 8, of which 7 were waited for; matrix products, arithmetic and copies ran while one was open for 12% of the time, Pallas kernels for 0%

commit v1 on v0

v1 whole, which is shorter than its diff:
```python
import jax
import jax.numpy as jnp
from jax import lax
from jax.experimental import pallas as pl
from jax.experimental.pallas import tpu as pltpu
from jax.sharding import Mesh, PartitionSpec as P

ROW = ("x", "core")
COL = ("y", "z")
ALL = ROW + COL
BLOCK = 512
F32 = jnp.float32
BF16 = jnp.bfloat16


def dot(a, b):
    return jnp.dot(a, b, preferred_element_type=F32)


def dot_tn(a, b):
    return lax.dot_general(a, b, (((0,), (0,)), ((), ())), preferred_element_type=F32)


def one_hot(index, shape, dim):
    spots = lax.broadcasted_iota(jnp.int32, shape, dim).astype(F32)
    return jnp.where(index == spots, 1.0, 0.0).astype(BF16)


def pick(index, value, shape):
    return jnp.broadcast_to(jnp.where(index == value, 1.0, 0.0), shape).astype(BF16)


def outgoing_kernel(ids_ref, feat_ref, out_ref):
    n = feat_ref.shape[0]
    cols = jnp.transpose(jnp.broadcast_to(ids_ref[...], (8, n)).astype(F32))
    out_ref[...] = dot(one_hot(cols[:, 0:1], (n, n), 1), feat_ref[...]).astype(BF16)


def encoder_kernel(neigh_ref, feat_ref, recv_ref, wself_ref, wneigh_ref, bias_ref, agg_ref, emb_ref):
    fanout, n = neigh_ref.shape
    cols = jnp.transpose(neigh_ref[...].astype(F32))
    spots = lax.broadcasted_iota(jnp.int32, (n, 2 * n), 1).astype(F32)
    count = jnp.zeros((n, 2 * n), F32)
    for k in range(fanout):
        count = count + jnp.where(cols[:, k : k + 1] == spots, 1.0, 0.0)
    count = count.astype(BF16)
    total = dot(count[:, :n], feat_ref[...]) + dot(count[:, n:], recv_ref[...])
    agg = (total / fanout).astype(BF16)
    agg_ref[...] = agg
    emb = dot(feat_ref[...], wself_ref[...]) + dot(agg, wneigh_ref[...]) + bias_ref[...]
    emb_ref[...] = emb.astype(BF16)


def decoder_kernel(
    seg_ref, fields_ref, es_ref, ed_ref, w1_ref, w1t_ref, bfirst_ref, w2_ref, b2_ref,
    logit_ref, sgrad_ref, dgrad_ref, gfirst_ref, vec_ref, sacc, dacc, xs,
):
    i = pl.program_id(0)
    d = es_ref.shape[2]
    parts = ed_ref.shape[0]

    @pl.when(i == 0)
    def _():
        sacc[...] = jnp.zeros_like(sacc)
        dacc[...] = jnp.zeros_like(dacc)
        gfirst_ref[...] = jnp.zeros_like(gfirst_ref)
        vec_ref[...] = jnp.zeros_like(vec_ref)

    rows = fields_ref[0]
    cols = jnp.transpose(rows)
    wide = (BLOCK, d)
    tall = (d, BLOCK)
    first = seg_ref[i, 0]
    last = seg_ref[i, 1]

    src_pick = one_hot(cols[:, 1:2], wide, 1)
    xs[...] = jnp.zeros_like(xs)

    def gather_src(o, carry):
        mask = pick(cols[:, 0:1], o.astype(F32), wide)
        xs[...] += dot(src_pick * mask, es_ref[o])
        return carry

    lax.fori_loop(first, last + 1, gather_src, 0)
    dst_pick = one_hot(cols[:, 3:4], wide, 1)
    xd_f = jnp.zeros(wide, F32)
    for h in range(parts):
        xd_f = xd_f + dot(dst_pick * pick(cols[:, 2:3], float(h), wide), ed_ref[h])
    x_src = xs[...].astype(BF16)
    x_dst = xd_f.astype(BF16)

    preact = dot(x_src, w1_ref[:d]) + dot(x_dst, w1_ref[d:]) + bfirst_ref[...]
    sig = jax.nn.sigmoid(preact)
    hidden = preact * sig
    w2 = w2_ref[...]
    logits = jnp.sum(hidden.astype(BF16).astype(F32) * w2, axis=1, keepdims=True) + b2_ref[0, 0]
    dlogit = jax.nn.sigmoid(logits) - cols[:, 4:5]
    dpre = dlogit * w2 * (sig * (1.0 + preact * (1.0 - sig)))
    dpre_b = dpre.astype(BF16)
    logit_ref[0] = jnp.transpose(jnp.broadcast_to(logits, (BLOCK, 128)))[0:1, :]
    vec_ref[1:2, :] += jnp.sum(dpre, axis=0, keepdims=True)
    vec_ref[2:3, :] += jnp.sum(hidden * dlogit, axis=0, keepdims=True)
    gfirst_ref[:d] += dot_tn(x_src, dpre_b)
    gfirst_ref[d:] += dot_tn(x_dst, dpre_b)
    back = dot(dpre_b, w1t_ref[...]).astype(BF16)
    back_src = back[:, :d]
    back_dst = back[:, d:]
    back_f = back_src.astype(F32) + back_dst.astype(F32)
    vec_ref[0:1, :] += jnp.sum(back_f, axis=0, keepdims=True)

    src_put = one_hot(rows[1:2, :], tall, 0)

    def scatter_src(o, carry):
        mask = pick(rows[0:1, :], o.astype(F32), tall)
        sacc[o] += dot(src_put * mask, back_src)
        return carry

    lax.fori_loop(first, last + 1, scatter_src, 0)
    dst_put = one_hot(rows[3:4, :], tall, 0)
    for h in range(parts):
        dacc[h] += dot(dst_put * pick(rows[2:3, :], float(h), tall), back_dst)

    @pl.when(i == pl.num_programs(0) - 1)
    def _():
        sgrad_ref[...] = sacc[...].astype(BF16)
        dgrad_ref[...] = dacc[...].astype(BF16)


def encoder_grad_kernel(fs_ref, as_ref, sg_ref, fd_ref, ad_ref, dg_ref, out_ref):
    i = pl.program_id(0)
    d = fs_ref.shape[1]

    @pl.when(i == 0)
    def _():
        out_ref[...] = jnp.zeros_like(out_ref)

    out_ref[:d] += dot_tn(fs_ref[...], sg_ref[...]) + dot_tn(fd_ref[...], dg_ref[...])
    out_ref[d:] += dot_tn(as_ref[...], sg_ref[...]) + dot_tn(ad_ref[...], dg_ref[...])


def params(mib=48):
    return pltpu.CompilerParams(vmem_limit_bytes=mib * 1024 * 1024)


def a2a(x, axes):
    return lax.all_to_all(x, axes, split_axis=0, concat_axis=0, tiled=True)


def to_all(x, axes, count):
    return a2a(jnp.broadcast_to(x[None], (count,) + x.shape), axes)


def per_device(
    features, neighbours, halo_ids, w_self, w_neigh, b_sage, w_first, b_first,
    w_second, b_second, src_owner, src_local, dst_index, labels,
):
    n, d = features.shape
    nx, nc, ny, nz = (lax.axis_size(a) for a in ALL)
    nrow, ncol = nx * nc, ny * nz
    edges = src_local.shape[2]
    blocks = edges // BLOCK

    f_col = lax.all_gather(lax.all_gather(features, "z"), "y")
    f_row = to_all(features, ROW, nrow)

    outgoing = pl.pallas_call(
        outgoing_kernel, out_shape=jax.ShapeDtypeStruct((n, d), BF16), compiler_params=params()
    )(halo_ids[0], features)
    received = a2a(outgoing.reshape(nrow, ncol, d), ROW)
    received = lax.all_to_all(received, COL, split_axis=1, concat_axis=1, tiled=True)

    key = ((src_owner[0, 0, :, 0] * n + src_local[0, 0]) << 12) | (dst_index[0, 0] << 1) | labels[0, 0]
    key, order = lax.sort((key, lax.iota(jnp.int32, edges)), num_keys=1)
    key = key.reshape(blocks, BLOCK)
    owner = key >> 20
    dst = key >> 1
    zero = jnp.zeros_like(key)
    fields = jnp.stack(
        [owner, (key >> 12) & 255, (dst >> 8) & 7, dst & 255, key & 1, zero, zero, zero], axis=1
    ).astype(F32)
    seg = jnp.stack([owner[:, 0], owner[:, -1]], axis=1)

    agg, embeds = pl.pallas_call(
        encoder_kernel,
        out_shape=(jax.ShapeDtypeStruct((n, d), BF16), jax.ShapeDtypeStruct((n, d), BF16)),
        compiler_params=params(),
    )(neighbours, features, received.reshape(nrow * ncol, d), w_self, w_neigh, b_sage[None])
    a_row = to_all(agg, ROW, nrow)
    a_col = lax.all_gather(lax.all_gather(agg, "z"), "y")

    def embed(f, a):
        e = dot(f.reshape(-1, d), w_self) + dot(a.reshape(-1, d), w_neigh) + b_sage
        return e.astype(BF16).reshape(-1, n, d)

    e_row = embed(f_row, a_row)
    e_col = embed(f_col, a_col)

    def whole(*shape):
        return pl.BlockSpec(shape, lambda i, s: (0,) * len(shape))

    logits, sgrad, dgrad, gfirst, vec = pl.pallas_call(
        decoder_kernel,
        grid_spec=pltpu.PrefetchScalarGridSpec(
            num_scalar_prefetch=1,
            grid=(blocks,),
            in_specs=[
                pl.BlockSpec((1, 8, BLOCK), lambda i, s: (i, 0, 0)),
                whole(ncol, n, d), whole(nrow, n, d), whole(2 * d, d), whole(d, 2 * d),
                whole(1, d), whole(1, d), pl.BlockSpec(memory_space=pltpu.SMEM),
            ],
            out_specs=[
                pl.BlockSpec((1, 1, BLOCK), lambda i, s: (i, 0, 0)),
                whole(ncol, n, d), whole(nrow, n, d), whole(2 * d, d), whole(8, d),
            ],
            scratch_shapes=[
                pltpu.VMEM((ncol, n, d), F32), pltpu.VMEM((nrow, n, d), F32), pltpu.VMEM((BLOCK, d), F32),
            ],
        ),
        out_shape=(
            jax.ShapeDtypeStruct((blocks, 1, BLOCK), F32),
            jax.ShapeDtypeStruct((ncol, n, d), BF16),
            jax.ShapeDtypeStruct((nrow, n, d), BF16),
            jax.ShapeDtypeStruct((2 * d, d), F32),
            jax.ShapeDtypeStruct((8, d), F32),
        ),
        compiler_params=params(),
    )(seg, fields, e_col, e_row, w_first, w_first.T, b_first[None], w_second.astype(F32)[None], b_second[None])

    logits = lax.sort((order, logits.reshape(edges)), num_keys=1)[1].reshape(1, 1, edges)

    from_y = a2a(sgrad.reshape(ny, nz, n, d), "y")
    part_y = jnp.sum(from_y.astype(F32), axis=0).astype(BF16)
    from_z = a2a(part_y, "z")
    from_row = a2a(dgrad, ROW)
    node_grad = jnp.sum(from_z.astype(F32), axis=0) + jnp.sum(from_row.astype(F32), axis=0)

    steps = 8
    big, small = ncol * n // steps, nrow * n // steps
    genc = pl.pallas_call(
        encoder_grad_kernel,
        grid=(steps,),
        in_specs=[pl.BlockSpec((big, d), lambda i: (i, 0))] * 3 + [pl.BlockSpec((small, d), lambda i: (i, 0))] * 3,
        out_specs=pl.BlockSpec((2 * d, d), lambda i: (0, 0)),
        out_shape=jax.ShapeDtypeStruct((2 * d, d), F32),
        compiler_params=params(),
    )(*(v.reshape(-1, d) for v in (f_col, a_col, sgrad, f_row, a_row, dgrad)))

    cut = 2 * d // nrow
    mixed = jnp.concatenate(
        [genc.reshape(nrow, cut, d), gfirst.reshape(nrow, cut, d), jnp.broadcast_to(vec[None], (nrow, 8, d))], axis=1
    )
    mixed = jnp.sum(a2a(mixed, ROW), axis=0)
    vec = mixed[2 * cut :]
    thin = cut // ncol
    over = jnp.concatenate(
        [mixed[:cut].reshape(ncol, thin, d), jnp.broadcast_to(vec[None, 0:1], (ncol, 1, d))], axis=1
    )
    over = jnp.sum(a2a(over, COL), axis=0)
    grad_bsage = over[thin]
    enc_cut = to_all(over[:thin], COL, ncol).reshape(cut, d)
    final = to_all(jnp.concatenate([enc_cut, mixed[cut : 2 * cut]], axis=0), ROW, nrow)
    enc = final[:, :cut].reshape(2 * d, d)
    dec = final[:, cut:].reshape(2 * d, d)
    return (
        embeds, logits, node_grad, enc[:d], enc[d:], grad_bsage, dec[None], vec[1:2], vec[2:3],
    )


def solution(mesh):
    fine = Mesh(mesh.devices.reshape(mesh.shape["row"] // 2, 2, mesh.shape["col"] // 8, 8), ALL)
    edge = P(ROW, COL, None)
    placed = (
        P(ALL, None), P(None, ALL), P(ALL, None, None),
        P(), P(), P(), P(), P(), P(), P(),
        P(ROW, COL, None, None), edge, edge, edge,
    )
    return jax.shard_map(
        per_device,
        mesh=fine,
        in_specs=placed,
        out_specs=(
            P(ALL, None), edge, P(ALL, None), P(), P(), P(),
            P(COL, None, None), P(COL, None), P(COL, None),
        ),
        check_vma=False,
    )
```

time: 876 us -> 488 us (0.56)
  waiting for transfers between devices: 534 us -> 211 us
  Pallas kernels: 0 us -> 98.5 us
  other arithmetic: 105 us -> 19.4 us
  local copies, waits for them, and re-layouts: 84.1 us -> 14.2 us
  matrix products: 31.8 us -> 18.4 us
    psum x2 -> x0, waiting for transfers between devices: 228 us -> none  [the longest x1 163 us: per_device(): encoder_sums = lax.psum((part_self, part_neigh, part_bsage), ('row', 'col'))]
    reduce_scatter x2 -> x0, waiting for transfers between devices: 222 us -> none  [the longest x1 222 us: per_device(): src_grad = lax.psum_scatter(src_acc, 'col', scatter_dimension=0, tiled=True)]
    all_to_all x2 -> x6, waiting for transfers between devices: 13.3 us -> 114 us  [a2a(): return lax.all_to_all(x, axes, split_axis=0, concat_axis=0, tiled=True)]
    pallas_call x0 -> x4, Pallas kernels: none -> 98.5 us  [the longest x1 87.4 us: per_device(): pl.pallas_call(decoder_kernel, grid_spec=pltpu.PrefetchScalarGridSpec(num...]
    scatter-add x2 -> x0, other arithmetic: 94.3 us -> none  [the longest x1 48.3 us: per_device(): src_acc = jnp.zeros((src_block.shape[0], feat_width), jnp.float32).at[blo...]
    psum x2 -> x0, blocking collectives: 87.7 us -> none  [the longest x1 74.7 us: per_device(): encoder_sums = lax.psum((part_self, part_neigh, part_bsage), ('row', 'col'))]
    all_to_all x0 -> x5, blocking collectives: none -> 84.9 us  [the longest x4 63.5 us: a2a(): return lax.all_to_all(x, axes, split_axis=0, concat_axis=0, tiled=True)]
    gather x4 -> x0, local copies, waits for them, and re-layouts: 76 us -> none  [the longest x1 33.6 us: per_device(): src_embed = src_block[block_rows]]
  transfers between devices with their start and end apart: 8 -> 10, of which waited for: 7 -> 10; matrix products, arithmetic and copies ran while one was open for 12% -> 7% of each run, Pallas kernels for 0% -> 0%
where the time goes in v1:
time: 488 us; the launch traced here: 487 us
  waiting for transfers between devices  211 us (43%)
  Pallas kernels  98.5 us (20%)
  blocking collectives  84.9 us (17%)
  starting transfers between devices  25 us (5%)
  other arithmetic  19.4 us (4%)
  matrix products  18.4 us (4%)
  between operations  14.8 us (3%)
  local copies, waits for them, and re-layouts  14.2 us (3%)
    all_to_all x6, waiting for transfers between devices, a2a(): return lax.all_to_all(x, axes, split_axis=0, concat_axis=0, tiled=True)  114 us
    pallas_call x1, Pallas kernels, per_device(): pl.pallas_call(decoder_kernel, grid_spec=pltpu.PrefetchScalarGridSpec(num...  87.4 us
    all_gather x2, waiting for transfers between devices, per_device(): a_col = lax.all_gather(lax.all_gather(agg, 'z'), 'y')  86.9 us
    all_to_all x4, blocking collectives, a2a(): return lax.all_to_all(x, axes, split_axis=0, concat_axis=0, tiled=True)  63.5 us
    all_to_all x6, starting transfers between devices, a2a(): return lax.all_to_all(x, axes, split_axis=0, concat_axis=0, tiled=True)  24.9 us
    all_to_all x1, blocking collectives, per_device(): lax.all_to_all(received, COL, split_axis=1, concat_axis=1, tiled=True)  21.4 us
    dot_general x4, matrix products, dot(): return jnp.dot(a, b, preferred_element_type=F32)  18.4 us
    all_gather x2, waiting for transfers between devices, per_device(): f_col = lax.all_gather(lax.all_gather(features, 'z'), 'y')  9.99 us
  transfers between devices with their start and end apart: 10, of which 10 were waited for; matrix products, arithmetic and copies ran while one was open for 7% of the time, Pallas kernels for 0%

profile of v1, /device:TPU:8, one launch (start us, length us, event | category | flops | bytes accessed | tf_op | source)
XLA Modules:
  0.0 486.6 jit_solution(16096239761157481919)
XLA Ops:
  9.9 10.2 %all_to_all.55 = bf16[8,32,256]{2,1,0:T(8,128)(2,1)S(1)} all-to-all(bf16[8,32,256]{2,1,0:T(8,128)(2,1)S(1)} %bitcast.54), channel_id=1, replica_groups=mesh['x'=4,'core'=2,'y'=4,'z'=8] {'x','core'}, dimensions={0} | all-to-all | bytes 262144 | tf_op jit(solution)/shard_map/all_to_all | solution.py:146
  20.3 21.4 %all_to_all.56 = bf16[8,32,256]{2,0,1:T(8,128)(2,1)S(1)} all-to-all(bf16[8,32,256]{2,0,1:T(8,128)(2,1)S(1)} %copy.40), channel_id=1, replica_groups=mesh['x'=4,'core'=2,'y'=4,'z'=8] {'y','z'}, dimensions={1} | all-to-all | bytes 262144 | tf_op jit(solution)/shard_map/all_to_all | solution.py:170
  45.8 1.7 shard_map.206
  47.6 4.3 all-gather.9.cloned.1.call-done
  51.9 40.7 %all-gather.13.cloned.1.call-done = bf16[2048,256]{1,0:T(8,128)(2,1)} async-done(((bf16[256,256]{1,0:T(8,128)(2,1)}), bf16[2048,256]{1,0:T(8,128)(2,1)}) %all-gather.13.cloned.1.call-update) | async-done | bytes 1048592 | tf_op jit(solution)/shard_map/all_gather | solution.py:189
  93.8 4.3 all-to-all-start.2
  98.1 15.9 %all-to-all-done.2 = bf16[8,256,256]{2,1,0:T(8,128)(2,1)S(1)} async-done(((bf16[8,256,256]{2,1,0:T(8,128)(2,1)}), bf16[8,256,256]{2,1,0:T(8,128)(2,1)S(1)}, u32[]{:S(2)}, u32[]{:S(2)}) %all-to-all-start.2) | async-done | bytes 1048608 | tf_op jit(solution)/shard_map/all_to_all | solution.py:146
  114.0 2.0 broadcast_in_dim.26
  116.0 3.7 all-to-all-start.3
  119.8 6.2 %sort.38 = (s32[8192]{0:T(1024)S(1)}, s32[8192]{0:T(1024)S(1)}) sort(s32[8192]{0:T(1024)S(1)} %or_or_fusion, s32[8192]{0:T(1024)S(1)} %iota.6), dimensions={0}, to_apply=%region_0.0 | sort | flops 106496 | bytes 131072 | tf_op jit(solution)/shard_map/sort | solution.py:173
  128.8 1.8 fusion.9
  130.5 4.9 %all-to-all-done.3 = bf16[8,256,256]{2,1,0:T(8,128)(2,1)S(1)} async-done(((bf16[8,256,256]{2,1,0:T(8,128)(2,1)}), bf16[8,256,256]{2,1,0:T(8,128)(2,1)S(1)}, u32[]{:S(2)}, u32[]{:S(2)}) %all-to-all-start.3) | async-done | bytes 1048608 | tf_op jit(solution)/shard_map/all_to_all | solution.py:146
  135.4 2.0 fusion.3
  137.5 5.7 %all-gather.11.cloned.1.call-done = bf16[32,256,256]{2,1,0:T(8,128)(2,1)} async-done(((bf16[8,256,256]{2,1,0:T(8,128)(2,1)}), bf16[32,256,256]{2,1,0:T(8,128)(2,1)}) %all-gather.11.cloned.1.call-update) | async-done | bytes 4194320 | tf_op jit(solution)/shard_map/all_gather | solution.py:163
  143.2 6.7 %fusion.8 = f32[8192,256]{1,0:T(8,128)} fusion(bf16[8192,256]{1,0:T(8,128)(2,1)} %bitcast.64, bf16[256,256]{1,0:T(8,128)(2,1)S(1)} %copy-done.4), kind=kOutput, calls=%fused_computation.24 | convolution fusion | flops 1073741824 | bytes 12713984 | tf_op jit(solution)/shard_map/dot_general | solution.py:17
  149.8 46.2 %all-gather.15.cloned.1.call-done = bf16[32,256,256]{2,1,0:T(8,128)(2,1)} async-done(((bf16[8,256,256]{2,1,0:T(8,128)(2,1)}), bf16[32,256,256]{2,1,0:T(8,128)(2,1)}) %all-gather.15.cloned.1.call-update) | async-done | bytes 4194320 | tf_op jit(solution)/shard_map/all_gather | solution.py:189
  196.1 7.9 %fusion.1 = bf16[8192,256]{1,0:T(8,128)(2,1)} fusion(f32[8192,256]{1,0:T(8,128)} %fusion.8, bf16[8192,256]{1,0:T(8,128)(2,1)} %bitcast.62, bf16[256,256]{1,0:T(8,128)(2,1)S(1)} %copy-done.6, f32[256]{0:T(256)S(1)} %copy-done.12), kind=kOutput, calls=%fused_computation.2 | convolution fusion | flops 1080033280 | bytes 16909312 | tf_op jit(solution)/shard_map/dot_general | solution.py:17
  204.0 87.4 %shard_map.207 = (f32[16,1,512]{2,1,0:T(1,128)S(1)}, bf16[32,256,256]{2,1,0:T(8,128)(2,1)}, bf16[8,256,256]{2,1,0:T(8,128)(2,1)}, f32[512,256]{1,0:T(8,128)S(1)}, f32[8,256]{1,0:T(8,128)S(1)}) custom-call(s32[16,2]{1,0:T(8,128)S(1)} %pad_add_fusion.seg_ref, f32[16,8,512]{2,1,0:T(8,128)S(1)} %copy-done.9, bf16[32,256,256]{2,1,0:T(8,128)(2,1)} %bitcast.61, ...), custom_call_target="tpu_custom_call" | custom-call | tf_op jit(solution)/shard_map/pallas_call | solution.py:201
  291.4 9.0 %shard_map.208 = f32[512,256]{1,0:T(8,128)S(1)} custom-call(bf16[8192,256]{1,0:T(8,128)(2,1)} %bitcast.65, bf16[8192,256]{1,0:T(8,128)(2,1)} %bitcast.63, bf16[8192,256]{1,0:T(8,128)(2,1)} %bitcast.66, bf16[2048,256]{1,0:T(8,128)(2,1)S(1)} %bitcast.47, bf16[2048,256]{1,0:T(8,128)(2,1)S(1)} %bitcast.49, bf16[2048,256]{1,0:T(8,128)(2,1)} %bitcast.29.dg_ref), custom_call_target="tpu_custom_call" | custom-call | tf_op jit(solution)/shard_map/pallas_call | solution.py:239
  300.5 20.9 %all_to_all.57 = f32[8,136,256]{2,1,0:T(8,128)S(1)} all-to-all(f32[8,136,256]{2,1,0:T(8,128)S(1)} %pad_maximum_fusion), channel_id=1, replica_groups=mesh['x'=4,'core'=2,'y'=4,'z'=8] {'x','core'}, dimensions={0} | all-to-all | bytes 2228224 | tf_op jit(solution)/shard_map/all_to_all | solution.py:146
  322.3 18.7 %all_to_all.58 = f32[32,3,256]{2,1,0:T(4,128)S(1)} all-to-all(f32[32,3,256]{2,1,0:T(4,128)S(1)} %pad_maximum_fusion.1), channel_id=1, replica_groups=mesh['x'=4,'core'=2,'y'=4,'z'=8] {'y','z'}, dimensions={0} | all-to-all | bytes 196608 | tf_op jit(solution)/shard_map/all_to_all | solution.py:146
  341.0 3.6 all-to-all-start.6
  344.6 15.8 %all-to-all-done.6 = bf16[8,256,256]{2,1,0:T(8,128)(2,1)S(1)} async-done(((bf16[8,256,256]{2,1,0:T(8,128)(2,1)}), bf16[8,256,256]{2,1,0:T(8,128)(2,1)S(1)}, u32[]{:S(2)}, u32[]{:S(2)}) %all-to-all-start.6) | async-done | bytes 1048608 | tf_op jit(solution)/shard_map/all_to_all | solution.py:146
  360.5 13.6 %all_to_all.59 = f32[32,2,256]{2,1,0:T(2,128)S(1)} all-to-all(f32[32,2,256]{2,1,0:T(2,128)S(1)} %broadcast_in_dim.64), channel_id=1, replica_groups=mesh['x'=4,'core'=2,'y'=4,'z'=8] {'y','z'}, dimensions={0} | all-to-all | bytes 131072 | tf_op jit(solution)/shard_map/all_to_all | solution.py:146
  374.1 6.2 %all-to-all-start.4 = ((bf16[4,8,256,256]{3,2,1,0:T(8,128)(2,1)}), bf16[4,8,256,256]{3,2,1,0:T(8,128)(2,1)}, u32[]{:S(2)}, u32[]{:S(2)}) async-start(bf16[4,8,256,256]{3,2,1,0:T(8,128)(2,1)} %bitcast.67), calls=%async_computation.4 | async-start | bytes 8388608 | tf_op jit(solution)/shard_map/all_to_all | solution.py:146
  380.3 46.0 %all-to-all-done.4 = bf16[4,8,256,256]{3,2,1,0:T(8,128)(2,1)} async-done(((bf16[4,8,256,256]{3,2,1,0:T(8,128)(2,1)}), bf16[4,8,256,256]{3,2,1,0:T(8,128)(2,1)}, u32[]{:S(2)}, u32[]{:S(2)}) %all-to-all-start.4) | async-done | bytes 4194336 | tf_op jit(solution)/shard_map/all_to_all | solution.py:146
  427.4 3.6 all-to-all-start.10
  431.0 4.1 reduce_sum.48
  435.1 11.8 %all-to-all-done.10 = f32[8,128,256]{2,1,0:T(8,128)S(1)} async-done(((f32[8,128,256]{2,1,0:T(8,128)}), f32[8,128,256]{2,1,0:T(8,128)S(1)}, u32[]{:S(2)}, u32[]{:S(2)}) %all-to-all-start.10) | async-done | bytes 1048608 | tf_op jit(solution)/shard_map/all_to_all | solution.py:146
  446.9 3.6 all-to-all-start.5
  450.5 6.9 %sort.39 = (s32[8192]{0:T(1024)}, f32[8192]{0:T(1024)}, s32[8192]{0:T(1024)}) sort(s32[8192]{0:T(1024)S(1)} %get-tuple-element.22, f32[8192]{0:T(1024)S(1)} %bitcast.56, s32[8192]{0:T(1024)S(1)} %iota.7), dimensions={0}, to_apply=%region_1.0 | sort | flops 106496 | bytes 196608 | tf_op jit(solution)/shard_map/sort | solution.py:229
  459.8 19.4 %all-to-all-done.5 = bf16[8,256,256]{2,1,0:T(8,128)(2,1)S(1)} async-done(((bf16[8,256,256]{2,1,0:T(8,128)(2,1)}), bf16[8,256,256]{2,1,0:T(8,128)(2,1)S(1)}, u32[]{:S(2)}, u32[]{:S(2)}) %all-to-all-start.5) | async-done | bytes 1048608 | tf_op jit(solution)/shard_map/all_to_all | solution.py:146
  (89 shorter events, 15.7 us)
Async XLA Ops:
  7.2 85.5 %copy-start.2 = (bf16[256,256]{1,0:T(8,128)(2,1)S(1)}, bf16[256,256]{1,0:T(8,128)(2,1)}, u32[]{:S(2)}) copy-start(bf16[256,256]{1,0:T(8,128)(2,1)} %feat_ref.3) | copy-start | bytes 393220
  7.2 44.7 %all-gather.9.cloned.1.call-start = ((), (), s32[]{:S(2)}) async-start(), calls=%async_computation.11 | async-start | bytes 1179648 | tf_op jit(solution)/shard_map/all_gather | solution.py:163
  7.9 84.7 %all-gather.13.cloned.1.call-start = ((), (), s32[]{:S(2)}) async-start(), calls=%async_computation.13 | async-start | bytes 1179648 | tf_op jit(solution)/shard_map/all_gather | solution.py:189
  8.0 0.9 copy-start
  8.9 0.7 copy-start.14
  9.6 88.5 %copy-start.18 = (s32[1,1,8192]{2,1,0:T(1,128)S(1)}, s32[1,1,8192]{2,1,0:T(1,128)}, u32[]{:S(2)}) copy-start(s32[1,1,8192]{2,1,0:T(1,128)} %param.26) | copy-start | bytes 98308
  9.6 88.5 %copy-start.19 = (s32[1,1,8192,1]{2,3,1,0:T(1,128)S(1)}, s32[1,1,8192,1]{2,3,1,0:T(1,128)}, u32[]{:S(2)}) copy-start(s32[1,1,8192,1]{2,3,1,0:T(1,128)} %param.24) | copy-start | bytes 98308
  41.7 0.9 copy-start.1
  42.6 0.9 copy-start.3
  43.5 0.9 copy-start.5
  44.4 0.7 copy-start.11
  45.1 0.7 copy-start.13
  47.5 95.6 %all-gather.11.cloned.1.call-start = ((), (), s32[]{:S(2)}) async-start(), calls=%async_computation.12 | async-start | bytes 5242880 | tf_op jit(solution)/shard_map/all_gather | solution.py:163
  51.9 67.9 %copy-start.16 = (s32[1,1,8192]{2,1,0:T(1,128)S(1)}, s32[1,1,8192]{2,1,0:T(1,128)}, u32[]{:S(2)}) copy-start(s32[1,1,8192]{2,1,0:T(1,128)} %param.27) | copy-start | bytes 98308
  51.9 67.9 %copy-start.17 = (s32[1,1,8192]{2,1,0:T(1,128)S(1)}, s32[1,1,8192]{2,1,0:T(1,128)}, u32[]{:S(2)}) copy-start(s32[1,1,8192]{2,1,0:T(1,128)} %param.25) | copy-start | bytes 98308
  51.9 144.2 %all-gather.15.cloned.1.call-start = ((), (), s32[]{:S(2)}) async-start(), calls=%async_computation.14 | async-start | bytes 5242880 | tf_op jit(solution)/shard_map/all_gather | solution.py:189
  92.7 34.4 %copy-start.7 = (bf16[512,256]{1,0:T(8,128)(2,1)S(1)}, bf16[512,256]{1,0:T(8,128)(2,1)}, u32[]{:S(2)}) copy-start(bf16[512,256]{1,0:T(8,128)(2,1)} %w1_ref.1) | copy-start | bytes 786436
  92.7 35.2 %copy-start.20 = (bf16[256]{0:T(256)(128)(2,1)S(1)}, bf16[256]{0:T(256)(128)(2,1)}, u32[]{:S(2)}) copy-start(bf16[256]{0:T(256)(128)(2,1)} %param.22) | copy-start | bytes 1540
  92.7 36.0 %copy-start.4 = (bf16[256,256]{1,0:T(8,128)(2,1)S(1)}, bf16[256,256]{1,0:T(8,128)(2,1)}, u32[]{:S(2)}) copy-start(bf16[256,256]{1,0:T(8,128)(2,1)} %wself_ref.1) | copy-start | bytes 393220
  93.8 20.2 %all-to-all-start.2 = ((bf16[8,256,256]{2,1,0:T(8,128)(2,1)}), bf16[8,256,256]{2,1,0:T(8,128)(2,1)S(1)}, u32[]{:S(2)}, u32[]{:S(2)}) async-start(bf16[8,256,256]{2,1,0:T(8,128)(2,1)} %broadcast_in_dim.25), calls=%async_computation.2 | async-start | bytes 2097152 | tf_op jit(solution)/shard_map/all_to_all | solution.py:146
  98.1 37.3 %copy-start.6 = (bf16[256,256]{1,0:T(8,128)(2,1)S(1)}, bf16[256,256]{1,0:T(8,128)(2,1)}, u32[]{:S(2)}) copy-start(bf16[256,256]{1,0:T(8,128)(2,1)} %wneigh_ref.1) | copy-start | bytes 393220
  98.1 37.3 %copy-start.12 = (f32[256]{0:T(256)S(1)}, f32[256]{0:T(256)}, u32[]{:S(2)}) copy-start(f32[256]{0:T(256)} %param.19) | copy-start | bytes 3076
  116.0 19.5 %all-to-all-start.3 = ((bf16[8,256,256]{2,1,0:T(8,128)(2,1)}), bf16[8,256,256]{2,1,0:T(8,128)(2,1)S(1)}, u32[]{:S(2)}, u32[]{:S(2)}) async-start(bf16[8,256,256]{2,1,0:T(8,128)(2,1)} %broadcast_in_dim.26), calls=%async_computation.3 | async-start | bytes 2097152 | tf_op jit(solution)/shard_map/all_to_all | solution.py:146
  196.1 7.9 %copy-start.8 = (bf16[512,256]{1,0:T(8,128)(2,1)S(1)}, bf16[512,256]{1,0:T(8,128)(2,1)}, u32[]{:S(2)}) copy-start(bf16[512,256]{1,0:T(8,128)(2,1)} %w1_ref.1) | copy-start | bytes 786436
  196.1 7.9 %copy-start.9 = (f32[16,8,512]{2,1,0:T(8,128)S(1)}, f32[16,8,512]{2,1,0:T(8,128)}, u32[]{:S(2)}) copy-start(f32[16,8,512]{2,1,0:T(8,128)} %convert_element_type.18.fields_ref) | copy-start | bytes 786436
  196.1 7.9 %copy-start.10 = (bf16[512,256]{0,1:T(8,128)(2,1)S(1)}, bf16[512,256]{0,1:T(8,128)(2,1)}, u32[]{:S(2)}) copy-start(bf16[512,256]{0,1:T(8,128)(2,1)} %copy.42) | copy-start | bytes 786436
  196.1 7.9 %copy-start.15 = (f32[256]{0:T(256)S(1)}, f32[256]{0:T(256)}, u32[]{:S(2)}) copy-start(f32[256]{0:T(256)} %param.21) | copy-start | bytes 3076
  341.0 19.4 %all-to-all-start.6 = ((bf16[8,256,256]{2,1,0:T(8,128)(2,1)}), bf16[8,256,256]{2,1,0:T(8,128)(2,1)S(1)}, u32[]{:S(2)}, u32[]{:S(2)}) async-start(bf16[8,256,256]{2,1,0:T(8,128)(2,1)} %get-tuple-element.28), calls=%async_computation.6 | async-start | bytes 2097152 | tf_op jit(solution)/shard_map/all_to_all | solution.py:146
  374.1 52.3 %all-to-all-start.4 = ((bf16[4,8,256,256]{3,2,1,0:T(8,128)(2,1)}), bf16[4,8,256,256]{3,2,1,0:T(8,128)(2,1)}, u32[]{:S(2)}, u32[]{:S(2)}) async-start(bf16[4,8,256,256]{3,2,1,0:T(8,128)(2,1)} %bitcast.67), calls=%async_computation.4 | async-start | bytes 8388608 | tf_op jit(solution)/shard_map/all_to_all | solution.py:146
  427.4 19.4 %all-to-all-start.10 = ((f32[8,128,256]{2,1,0:T(8,128)}), f32[8,128,256]{2,1,0:T(8,128)S(1)}, u32[]{:S(2)}, u32[]{:S(2)}) async-start(f32[8,128,256]{2,1,0:T(8,128)} %broadcast_in_dim.65), calls=%async_computation.10 | async-start | bytes 2097152 | tf_op jit(solution)/shard_map/all_to_all | solution.py:146
  446.9 32.3 %all-to-all-start.5 = ((bf16[8,256,256]{2,1,0:T(8,128)(2,1)}), bf16[8,256,256]{2,1,0:T(8,128)(2,1)S(1)}, u32[]{:S(2)}, u32[]{:S(2)}) async-start(bf16[8,256,256]{2,1,0:T(8,128)(2,1)} %reduce_sum.48), calls=%async_computation.5 | async-start | bytes 2097152 | tf_op jit(solution)/shard_map/all_to_all | solution.py:146
Sparse Core Ops, SparseCore 0:
  9.8 41.9 all-gather.8
  54.2 38.3 all-gather.12
  94.5 48.6 all-gather.10
  144.8 51.1 all-gather.14
